TPU v7x, 128 devices: a whole 4x4x4 slice. The times are simulated.
128 devices in a mesh: row: 16 (over y_lo, x, core), col: 8 (over z, y_hi).
Axes of the slice: x: 4, y: 4 (y_hi: 2, y_lo: 2; y = y_hi * 2 + y_lo), z: 4, core: 2. Of those that a mesh axis runs over, the one named last changes fastest.
Arguments:
- amplitudes: float32 [65536, 256], P(None, ('row', 'col')), may hold values from -24 to 24
- integrals: float32 [11264, 65536], P('row', 'col'), may hold values from -0.0234375 to 0.0234375
Outputs:
- ladder: float32 [11264, 256], P('row', 'col')
All inputs are finite; a program needn't handle non-finite values.
Results may differ from a plain program's by a relative error of at most 0.00007.
Values sent between devices are 32-bit elements; how exact they have to be, the bound alone decides.
A program may use at most 128 MiB of HBM per device.

v0:
```python
import jax
import jax.numpy as jnp
from jax import lax
from jax.sharding import PartitionSpec as P


def per_device(amplitudes, integrals):
    cd_panel = lax.all_to_all(amplitudes, "col", split_axis=0, concat_axis=1, tiled=True)
    partial_value = jnp.dot(
        integrals,
        lax.all_gather(cd_panel, "row", axis=1, tiled=True),
        preferred_element_type=jnp.float32,
        precision=lax.Precision.HIGHEST,
    )
    contracted = lax.psum_scatter(partial_value, "col", scatter_dimension=1, tiled=True)
    return 0.5 * contracted


def solution(mesh):
    return jax.shard_map(
        per_device,
        mesh=mesh,
        in_specs=(P(None, ("row", "col")), P("row", "col")),
        out_specs=P("row", "col"),
        check_vma=False,
    )
```

profile of v0, /device:TPU:4, one launch (start us, length us, event | category | flops | bytes accessed | tf_op | source)
XLA Modules:
  0.0 186.1 jit_solution(2681053563336530217)
XLA Ops:
  6.5 0.0 all-gather.2.cloned.1.call-start
  6.5 19.5 %all_to_all.19 = f32[8,8192,2]{1,2,0:T(2,128)S(1)} all-to-all(f32[8,8192,2]{1,2,0:T(2,128)} %bitcast.7), channel_id=1, replica_groups=mesh['row'=16,'col'=8] {'col'}, dimensions={0} | all-to-all | bytes 1048576 | tf_op jit(solution)/shard_map/all_to_all | solution.py:8
  26.1 1.2 all_to_all.17
  27.3 0.0 all-gather.2.cloned.1.call-update
  27.3 0.0 reduce-scatter.2.cloned.1.call-start
  27.3 49.0 %all-gather.2.cloned.1.call-done = f32[8192,256]{0,1:T(8,128)} async-done(((f32[8192,16]{0,1:T(8,128)}), f32[8192,256]{0,1:T(8,128)}) %all-gather.2.cloned.1.call-update) | async-done | bytes 8388624 | tf_op jit(solution)/shard_map/all_gather | solution.py:11
  76.3 28.8 %fusion = f32[704,256]{0,1:T(8,128)} fusion(f32[704,8192]{1,0:T(8,128)} %param.3, f32[8192,256]{0,1:T(8,128)} %all-gather.2.cloned.1.call-done), kind=kOutput, calls=%fused_computation.1 | convolution fusion | flops 17716740096 | bytes 32178176 | tf_op jit(solution)/shard_map/dot_general | solution.py:9
  105.2 0.0 reduce-scatter.2.cloned.1.call-update
  105.2 72.6 %reduce-scatter.2.cloned.1.call-done = f32[704,32]{0,1:T(8,128)} async-done(((f32[704,256]{0,1:T(8,128)}), f32[704,32]{0,1:T(8,128)}) %reduce-scatter.2.cloned.1.call-update) | async-done | bytes 90128 | tf_op jit(solution)/shard_map/reduce_scatter | solution.py:15
  177.8 1.5 broadcast_multiply_fusion
Async XLA Ops:
  6.5 69.8 %all-gather.2.cloned.1.call-start = ((), (), s32[]{:S(2)}) async-start(), calls=%async_computation.2 | async-start | bytes 8912896 | tf_op jit(solution)/shard_map/all_gather | solution.py:11
  27.3 150.5 %reduce-scatter.2.cloned.1.call-start = ((), (), s32[]{:S(2)}) async-start(), calls=%async_computation.3 | async-start | bytes 884736 | tf_op jit(solution)/shard_map/reduce_scatter | solution.py:15
Sparse Core Ops, SparseCore 0:
  27.4 48.8 all-gather.1
  105.3 72.4 reduce-scatter.1
where the time goes:
time: 187 us; the launch traced here: 186 us
  waiting for transfers between devices  122 us (65%)
  matrix products  28.8 us (15%)
  blocking collectives  19.5 us (10%)
  between operations  13.4 us (7%)
    reduce_scatter x1, waiting for transfers between devices, per_device(): lax.psum_scatter(partial_value, 'col', scatter_dimension=1, tiled=True)  72.6 us
    all_gather x1, waiting for transfers between devices, per_device(): lax.all_gather(cd_panel, 'row', axis=1, tiled=True)  49 us
    dot_general x1, matrix products, per_device(): jnp.dot(integrals, lax.all_gather(cd_panel, 'row', axis=1, tiled=True), p...  28.8 us
    all_to_all x1, blocking collectives, per_device(): lax.all_to_all(amplitudes, 'col', split_axis=0, concat_axis=1, tiled=True)  19.5 us
  transfers between devices with their start and end apart: 2, of which 2 were waited for; matrix products, arithmetic and copies ran while one was open for 0% of the time, Pallas kernels for 0%

commit v1 on v0

v1 whole, which is shorter than its diff:
```python
import functools

import jax
import jax.numpy as jnp
from jax import lax
from jax.experimental import pallas as pl
from jax.experimental.pallas import tpu as pltpu
from jax.sharding import PartitionSpec as P

MESH = pl.DeviceIdType.MESH
BF = jnp.bfloat16
F32 = jnp.float32
NT = (((1,), (1,)), ((), ()))

K = 8192
AB = 704
M = 8
CK = K // M
N = 2 * M
TILES = CK // 128
STAGES = 3


def dot(a, b):
    return lax.dot_general(a, b, NT, preferred_element_type=F32)


def split(v):
    hi = v.astype(BF)
    return hi, (v - hi.astype(F32)).astype(BF)


def kernel(amp, integ, out, raw, panel, stage, ah, al, bs, acc, part, land,
           own_sem, a2a_send, a2a_recv, stage_sem, g_send, g_recv, c_recv, rs_send, rs_recv):
    row, col = lax.axis_index("row"), lax.axis_index("col")
    core = lax.rem(row, 2)
    x = lax.rem(row // 2, 4)
    q = row // 8
    z, yhi = col // 2, lax.rem(col, 2)
    cls = lax.rem(q + yhi, 2)

    def rowid(qq, xx, kk):
        return (qq * 4 + xx) * 2 + kk

    xr, xl = lax.rem(x + 1, 4), lax.rem(x + 3, 4)
    xo = lax.rem(x + 2, 4)
    right = (rowid(q, xr, core), col)
    left = (rowid(q, xl, core), col)
    across = (rowid(1 - q, x, core), col)
    sib = (rowid(q, x, 1 - core), col)

    def a2a_dev(step):
        c = lax.rem(col + step, 8)
        return (rowid(lax.rem(cls + lax.rem(c, 2), 2), x, core), c)

    def rs_dev(step):
        return (row, lax.rem(col + step, 8))

    barrier = pltpu.get_barrier_semaphore()

    def greet(dev):
        pl.semaphore_signal(barrier, inc=1, device_id=dev, device_id_type=MESH)

    for dev in (right, left, across, sib):
        greet(dev)
    for s in range(1, 8):
        greet(a2a_dev(s))
    for s in range(1, 8, 2):
        greet(rs_dev(s))
    src_slot = yhi * 4 + z

    def stage_copy(m):
        return pltpu.make_async_copy(integ.at[:, pl.ds(pl.multiple_of(m * CK, CK), CK)],
                                     stage.at[lax.rem(m, STAGES)], stage_sem.at[lax.rem(m, STAGES)])

    own_copies = []
    for m in range(M):
        cp = pltpu.make_async_copy(
            amp.at[pl.ds(pl.multiple_of(col * 2 * K // 128 + m * 2 * TILES, 8), 2 * TILES)],
            raw.at[m, pl.ds(pl.multiple_of(src_slot * 2 * TILES, 8), 2 * TILES)], own_sem.at[m])
        cp.start()
        own_copies.append(cp)
    for m in range(STAGES):
        stage_copy(m).start()
    pl.semaphore_wait(barrier, 15)

    @pl.loop(0, M)
    def _(m):
        for s in range(1, 8):
            c, dev = lax.rem(col + s, 8), a2a_dev(s)
            pltpu.make_async_remote_copy(
                src_ref=amp.at[pl.ds(pl.multiple_of(c * (2 * K // 128) + m * 2 * TILES, 8), 2 * TILES)],
                dst_ref=raw.at[m, pl.ds(pl.multiple_of(src_slot * 2 * TILES, 8), 2 * TILES)],
                send_sem=a2a_send.at[0], recv_sem=a2a_recv.at[m], device_id=dev, device_id_type=MESH,
            ).start()

    acc[...] = jnp.zeros_like(acc)

    def slot(c, xx, kk):
        return (c * 4 + xx) * 2 + kk

    def piece(i, sl, half=None):
        rows = pl.ds(pl.multiple_of(sl * 8, 8), 8)
        if half is None:
            return panel.at[i, rows]
        return panel.at[i, rows, pl.ds(half * (CK // 2), CK // 2)]

    def send(i, sl, dev, sem, half=None):
        ref = piece(i, sl, half)
        pltpu.make_async_remote_copy(src_ref=ref, dst_ref=ref, send_sem=g_send.at[i], recv_sem=sem,
                                     device_id=dev, device_id_type=MESH).start()

    def wait(i, sl, sem):
        ref = piece(i, sl)
        pltpu.make_async_remote_copy(src_ref=ref, dst_ref=ref, send_sem=g_send.at[i], recv_sem=sem,
                                     device_id=right, device_id_type=MESH).wait_recv()

    def share(i, sl):
        send(i, sl, sib, c_recv.at[i])

    own = slot(cls, x, core)

    def first(i):
        m = i
        ref = raw.at[m, pl.ds(0, 7 * 2 * TILES)]

        @pl.when(i < M)
        def _():
            pltpu.make_async_copy(amp.at[pl.ds(0, 2 * TILES)], raw.at[m, pl.ds(0, 2 * TILES)], own_sem.at[m]).wait()
            pltpu.make_async_remote_copy(src_ref=ref, dst_ref=ref, send_sem=a2a_send.at[0], recv_sem=a2a_recv.at[m],
                                         device_id=right, device_id_type=MESH).wait_recv()
            for t in range(TILES):
                for j in range(2):
                    panel[m + j * M, pl.ds(pl.multiple_of(own * 8, 8), 8), t * 128:(t + 1) * 128] = (
                        raw[m, pl.ds(2 * t + j, 8, stride=2 * TILES), :])

        send(i, own, right, g_recv.at[i, 0])
        send(i, own, left, g_recv.at[i, 1])
        send(i, own, across, g_recv.at[i, 2])
        share(i, own)

    def second(i):
        @pl.when(core == 0)
        def _():
            theirs = slot(1 - cls, x, 0)
            wait(i, theirs, g_recv.at[i, 2])
            send(i, theirs, right, g_recv.at[i, 3])
            send(i, theirs, left, g_recv.at[i, 4])
            share(i, theirs)

    def third(i):
        @pl.when(core == 0)
        def _():
            for c, s in ((cls, 0), (1 - cls, 3)):
                wait(i, slot(c, xl, 0), g_recv.at[i, s])
                send(i, slot(c, xl, 0), right, g_recv.at[i, 5 + s // 3], 0)
                share(i, slot(c, xl, 0))
                wait(i, slot(c, xr, 0), g_recv.at[i, s + 1])
                send(i, slot(c, xr, 0), left, g_recv.at[i, 5 + s // 3], 1)
                share(i, slot(c, xr, 0))

        @pl.when(core == 1)
        def _():
            wait(i, slot(cls, xl, 1), g_recv.at[i, 0])
            send(i, slot(cls, xl, 1), right, g_recv.at[i, 3], 0)
            send(i, slot(cls, xl, 1), across, g_recv.at[i, 4])
            share(i, slot(cls, xl, 1))
            wait(i, slot(cls, xr, 1), g_recv.at[i, 1])
            send(i, slot(cls, xr, 1), left, g_recv.at[i, 3], 1)
            send(i, slot(cls, xr, 1), across, g_recv.at[i, 5])
            share(i, slot(cls, xr, 1))

    def fourth(i):
        @pl.when(core == 0)
        def _():
            for c, s in ((cls, 5), (1 - cls, 6)):
                wait(i, slot(c, xo, 0), g_recv.at[i, s])
                share(i, slot(c, xo, 0))

        @pl.when(core == 1)
        def _():
            wait(i, slot(cls, xo, 1), g_recv.at[i, 3])
            send(i, slot(cls, xo, 1), across, g_recv.at[i, 6])
            share(i, slot(cls, xo, 1))
            for xx, s in ((x, 2), (xl, 4), (xr, 5)):
                wait(i, slot(1 - cls, xx, 1), g_recv.at[i, s])
                share(i, slot(1 - cls, xx, 1))

    def fifth(i):
        @pl.when(core == 1)
        def _():
            wait(i, slot(1 - cls, xo, 1), g_recv.at[i, 6])
            share(i, slot(1 - cls, xo, 1))

    def convert(m):
        st = lax.rem(m, STAGES)
        stage_copy(m).wait()

        @pl.loop(0, AB // 16, unroll=2)
        def _(r):
            rows = pl.ds(pl.multiple_of(r * 16, 16), 16)
            hi, lo = split(stage[st, rows, :])
            ah[m, rows, :] = hi
            al[m, rows, :] = lo

        @pl.when(m + STAGES < M)
        def _():
            stage_copy(m + STAGES).start()

    def compute(i):
        m = lax.rem(i, M)
        ref = panel.at[i, pl.ds(0, 64)]
        pltpu.make_async_remote_copy(src_ref=ref, dst_ref=ref, send_sem=g_send.at[i], recv_sem=c_recv.at[i],
                                     device_id=sib, device_id_type=MESH).wait_recv()
        mask = lax.rem(lax.broadcasted_iota(jnp.int32, (16, CK), 0), 8) < 4
        for xx in range(4):
            v0 = panel[i, xx * 16:xx * 16 + 16, :]
            v1 = panel[i, 64 + xx * 16:64 + xx * 16 + 16, :]
            for y, v in ((0, jnp.where(mask, v0, v1)), (1, jnp.where(mask, v1, v0))):
                hi, lo = split(v)
                at = y * 64 + xx * 16
                bs[at:at + 16, :] = hi
                bs[128 + at:128 + at + 16, :] = lo
        for a0, a1 in ((0, 352), (352, 704)):
            acc[a0:a1, :] += dot(ah[m, a0:a1, :], bs[...])
            acc[a0:a1, 0:128] += dot(al[m, a0:a1, :], bs[0:128, :])

    def finish(h):
        part[h, :, :] = (acc[:, 0:128] + acc[:, 128:256]).T
        acc[...] = jnp.zeros_like(acc)
        for s in range(1, 8):
            c = lax.rem(col + s, 8)
            pltpu.make_async_remote_copy(
                src_ref=part.at[h, pl.ds(pl.multiple_of(c * 16, 16), 16)], dst_ref=land.at[h, col],
                send_sem=rs_send.at[h], recv_sem=rs_recv.at[h], device_id=rs_dev(s), device_id_type=MESH).start()
        land[h, col, :, :] = part[h, pl.ds(pl.multiple_of(col * 16, 16), 16), :]

    LAG = 5

    @pl.loop(0, N + LAG)
    def _(i):
        @pl.when(i < N)
        def _():
            first(i)

        @pl.when((i >= 1) & (i < N + 1))
        def _():
            second(i - 1)

        @pl.when((i >= 2) & (i < N + 2))
        def _():
            third(i - 2)

        @pl.when((i >= 3) & (i < N + 3))
        def _():
            fourth(i - 3)

        @pl.when((i >= 4) & (i < N + 4))
        def _():
            fifth(i - 4)

        @pl.when(i < M)
        def _():
            convert(i)

        @pl.when(i >= LAG)
        def _():
            compute(i - LAG)

        @pl.when(i == M - 1 + LAG)
        def _():
            finish(0)

        @pl.when(i == N - 1 + LAG)
        def _():
            finish(1)

    for h in range(2):
        ref = land.at[h, pl.ds(0, 7)]
        pltpu.make_async_remote_copy(src_ref=ref, dst_ref=ref, send_sem=rs_send.at[h], recv_sem=rs_recv.at[h],
                                     device_id=right, device_id_type=MESH).wait_recv()
        total = land[h, 0]
        for c in range(1, 8):
            total += land[h, c]
        total = 0.5 * total
        for kk in range(2):
            for yy in range(2):
                for zz in range(4):
                    r = kk * 16 + zz * 4 + yy * 2 + h
                    s = kk * 8 + yy * 4 + zz
                    out[r:r + 1, :] = total[s:s + 1, :]

    ref = raw.at[pl.ds(0, 7)]
    pltpu.make_async_remote_copy(src_ref=ref, dst_ref=ref, send_sem=a2a_send.at[0], recv_sem=a2a_recv.at[0],
                                 device_id=right, device_id_type=MESH).wait_send()

    @pl.loop(0, N)
    def _(i):
        ref = panel.at[i, pl.ds(0, 120)]
        pltpu.make_async_remote_copy(src_ref=ref, dst_ref=ref, send_sem=g_send.at[i], recv_sem=c_recv.at[i],
                                     device_id=right, device_id_type=MESH).wait_send()

    for h in range(2):
        ref = land.at[h, pl.ds(0, 7)]
        pltpu.make_async_remote_copy(src_ref=ref, dst_ref=ref, send_sem=rs_send.at[h], recv_sem=rs_recv.at[h],
                                     device_id=right, device_id_type=MESH).wait_send()


def per_device(amplitudes, integrals):
    amp = amplitudes.reshape(512, 128, 2).transpose(0, 2, 1).reshape(1024, 128)
    dma = pltpu.SemaphoreType.DMA
    out = pl.pallas_call(
        kernel,
        out_shape=jax.ShapeDtypeStruct((32, AB), F32),
        in_specs=[pl.BlockSpec(memory_space=pl.ANY)] * 2,
        out_specs=pl.BlockSpec(memory_space=pltpu.VMEM),
        scratch_shapes=[
            pltpu.VMEM((M, 8 * 2 * TILES, 128), F32),
            pltpu.VMEM((N, 128, CK), F32),
            pltpu.VMEM((STAGES, AB, CK), F32),
            pltpu.VMEM((M, AB, CK), BF),
            pltpu.VMEM((M, AB, CK), BF),
            pltpu.VMEM((256, CK), BF),
            pltpu.VMEM((AB, 256), F32),
            pltpu.VMEM((2, 128, AB), F32),
            pltpu.VMEM((2, 8, 16, AB), F32),
            dma((M,)), dma((1,)), dma((M,)), dma((STAGES,)),
            dma((N,)), dma((N, 7)), dma((N,)), dma((2,)), dma((2,)),
        ],
        compiler_params=pltpu.CompilerParams(collective_id=0, has_side_effects=True, vmem_limit_bytes=60 * 2**20),
        cost_estimate=pl.CostEstimate(flops=2 * AB * K * 256, bytes_accessed=4 * AB * K, transcendentals=0),
    )(amp, integrals)
    return out.T


def solution(mesh):
    return jax.shard_map(
        per_device,
        mesh=mesh,
        in_specs=(P(None, ("row", "col")), P("row", "col")),
        out_specs=P("row", "col"),
        check_vma=False,
    )
```

time: 187 us -> 80.5 us (0.43)
  waiting for transfers between devices: 122 us -> 0 us
  Pallas kernels: 0 us -> 77.4 us
  matrix products: 28.8 us -> 0 us
  blocking collectives: 19.5 us -> 0 us
  between operations: 13.4 us -> 0.01 us
    pallas_call x0 -> x1, Pallas kernels: none -> 77.4 us  [per_device(): pl.pallas_call(kernel, out_shape=jax.ShapeDtypeStruct((32, AB), F32), in_...]
    reduce_scatter x1 -> x0, waiting for transfers between devices: 72.6 us -> none  [per_device(): lax.psum_scatter(partial_value, 'col', scatter_dimension=1, tiled=True)]
    all_gather x1 -> x0, waiting for transfers between devices: 49 us -> none  [per_device(): lax.all_gather(cd_panel, 'row', axis=1, tiled=True)]
    dot_general x1 -> x0, matrix products: 28.8 us -> none  [per_device(): jnp.dot(integrals, lax.all_gather(cd_panel, 'row', axis=1, tiled=True), p...]
    all_to_all x1 -> x0, blocking collectives: 19.5 us -> none  [per_device(): lax.all_to_all(amplitudes, 'col', split_axis=0, concat_axis=1, tiled=True)]
  transfers between devices with their start and end apart: 2 -> 0, of which waited for: 2 -> 0; matrix products, arithmetic and copies ran while one was open for 0% -> 0% of each run, Pallas kernels for 0% -> 0%
where the time goes in v1:
time: 80.5 us; the launch traced here: 79 us
  Pallas kernels  77.4 us (96%)
  local copies, waits for them, and re-layouts  1.54 us (2%)
    pallas_call x1, Pallas kernels, per_device(): pl.pallas_call(kernel, out_shape=jax.ShapeDtypeStruct((32, AB), F32), in_...  77.4 us

profile of v1, /device:TPU:4, one launch (start us, length us, event | category | flops | bytes accessed | tf_op | source)
XLA Modules:
  0.0 79.0 jit_solution(11353486585416604480)
XLA Ops:
  0.0 77.4 %shard_map.28 = f32[32,704]{1,0:T(8,128)} custom-call(f32[1024,128]{1,0:T(8,128)} %bitcast.6, f32[704,8192]{1,0:T(8,128)} %integ.1), custom_call_target="tpu_custom_call" | custom-call | flops 2952790016 | bytes 23068672 | tf_op jit(solution)/shard_map/pallas_call | solution.py:312
  77.4 1.5 %copy.5 = f32[704,32]{0,1:T(8,128)} copy(f32[704,32]{0,1:T(8,128)} %bitcast.7) | data formatting | bytes 180224

commit v2 on v1

--- a/solution.py
+++ b/solution.py
@@ -19,6 +19,8 @@
 N = 2 * M
 TILES = CK // 128
 STAGES = 3
+LAGS = (3, 6, 9, 12, 13)
+EVERY = 99
 
 
 def dot(a, b):
@@ -50,11 +52,16 @@
     sib = (rowid(q, x, 1 - core), col)
 
     def a2a_dev(step):
-        c = lax.rem(col + step, 8)
+        c = partner(step)
         return (rowid(lax.rem(cls + lax.rem(c, 2), 2), x, core), c)
 
+    FAR_FIRST = (5, 3, 7, 1, 4, 2, 6)
+
+    def partner(step):
+        return lax.rem(z + step // 2, 4) * 2 + lax.rem(yhi + step, 2)
+
     def rs_dev(step):
-        return (row, lax.rem(col + step, 8))
+        return (row, partner(step))
 
     barrier = pltpu.get_barrier_semaphore()
 
@@ -86,8 +93,8 @@
 
     @pl.loop(0, M)
     def _(m):
-        for s in range(1, 8):
-            c, dev = lax.rem(col + s, 8), a2a_dev(s)
+        for s in FAR_FIRST:
+            c, dev = partner(s), a2a_dev(s)
             pltpu.make_async_remote_copy(
                 src_ref=amp.at[pl.ds(pl.multiple_of(c * (2 * K // 128) + m * 2 * TILES, 8), 2 * TILES)],
                 dst_ref=raw.at[m, pl.ds(pl.multiple_of(src_slot * 2 * TILES, 8), 2 * TILES)],
@@ -119,6 +126,12 @@
         send(i, sl, sib, c_recv.at[i])
 
     own = slot(cls, x, core)
+
+    def y_first(i):
+        return (core == 0) | (lax.rem(i, EVERY) == EVERY - 1)
+
+    def x_first(i):
+        return (core == 1) & (lax.rem(i, EVERY) != EVERY - 1)
 
     def first(i):
         m = i
@@ -140,57 +153,57 @@
         share(i, own)
 
     def second(i):
-        @pl.when(core == 0)
-        def _():
-            theirs = slot(1 - cls, x, 0)
+        @pl.when(y_first(i))
+        def _():
+            theirs = slot(1 - cls, x, core)
             wait(i, theirs, g_recv.at[i, 2])
             send(i, theirs, right, g_recv.at[i, 3])
             send(i, theirs, left, g_recv.at[i, 4])
             share(i, theirs)
 
     def third(i):
-        @pl.when(core == 0)
+        @pl.when(y_first(i))
         def _():
             for c, s in ((cls, 0), (1 - cls, 3)):
-                wait(i, slot(c, xl, 0), g_recv.at[i, s])
-                send(i, slot(c, xl, 0), right, g_recv.at[i, 5 + s // 3], 0)
-                share(i, slot(c, xl, 0))
-                wait(i, slot(c, xr, 0), g_recv.at[i, s + 1])
-                send(i, slot(c, xr, 0), left, g_recv.at[i, 5 + s // 3], 1)
-                share(i, slot(c, xr, 0))
-
-        @pl.when(core == 1)
-        def _():
-            wait(i, slot(cls, xl, 1), g_recv.at[i, 0])
-            send(i, slot(cls, xl, 1), right, g_recv.at[i, 3], 0)
-            send(i, slot(cls, xl, 1), across, g_recv.at[i, 4])
-            share(i, slot(cls, xl, 1))
-            wait(i, slot(cls, xr, 1), g_recv.at[i, 1])
-            send(i, slot(cls, xr, 1), left, g_recv.at[i, 3], 1)
-            send(i, slot(cls, xr, 1), across, g_recv.at[i, 5])
-            share(i, slot(cls, xr, 1))
+                wait(i, slot(c, xl, core), g_recv.at[i, s])
+                send(i, slot(c, xl, core), right, g_recv.at[i, 5 + s // 3], 0)
+                share(i, slot(c, xl, core))
+                wait(i, slot(c, xr, core), g_recv.at[i, s + 1])
+                send(i, slot(c, xr, core), left, g_recv.at[i, 5 + s // 3], 1)
+                share(i, slot(c, xr, core))
+
+        @pl.when(x_first(i))
+        def _():
+            wait(i, slot(cls, xl, core), g_recv.at[i, 0])
+            send(i, slot(cls, xl, core), right, g_recv.at[i, 3], 0)
+            send(i, slot(cls, xl, core), across, g_recv.at[i, 4])
+            share(i, slot(cls, xl, core))
+            wait(i, slot(cls, xr, core), g_recv.at[i, 1])
+            send(i, slot(cls, xr, core), left, g_recv.at[i, 3], 1)
+            send(i, slot(cls, xr, core), across, g_recv.at[i, 5])
+            share(i, slot(cls, xr, core))
 
     def fourth(i):
-        @pl.when(core == 0)
+        @pl.when(y_first(i))
         def _():
             for c, s in ((cls, 5), (1 - cls, 6)):
-                wait(i, slot(c, xo, 0), g_recv.at[i, s])
-                share(i, slot(c, xo, 0))
-
-        @pl.when(core == 1)
-        def _():
-            wait(i, slot(cls, xo, 1), g_recv.at[i, 3])
-            send(i, slot(cls, xo, 1), across, g_recv.at[i, 6])
-            share(i, slot(cls, xo, 1))
+                wait(i, slot(c, xo, core), g_recv.at[i, s])
+                share(i, slot(c, xo, core))
+
+        @pl.when(x_first(i))
+        def _():
+            wait(i, slot(cls, xo, core), g_recv.at[i, 3])
+            send(i, slot(cls, xo, core), across, g_recv.at[i, 6])
+            share(i, slot(cls, xo, core))
             for xx, s in ((x, 2), (xl, 4), (xr, 5)):
-                wait(i, slot(1 - cls, xx, 1), g_recv.at[i, s])
-                share(i, slot(1 - cls, xx, 1))
+                wait(i, slot(1 - cls, xx, core), g_recv.at[i, s])
+                share(i, slot(1 - cls, xx, core))
 
     def fifth(i):
-        @pl.when(core == 1)
-        def _():
-            wait(i, slot(1 - cls, xo, 1), g_recv.at[i, 6])
-            share(i, slot(1 - cls, xo, 1))
+        @pl.when(x_first(i))
+        def _():
+            wait(i, slot(1 - cls, xo, core), g_recv.at[i, 6])
+            share(i, slot(1 - cls, xo, core))
 
     def convert(m):
         st = lax.rem(m, STAGES)
@@ -228,50 +241,39 @@
     def finish(h):
         part[h, :, :] = (acc[:, 0:128] + acc[:, 128:256]).T
         acc[...] = jnp.zeros_like(acc)
-        for s in range(1, 8):
-            c = lax.rem(col + s, 8)
+        for s in FAR_FIRST:
+            c = partner(s)
             pltpu.make_async_remote_copy(
                 src_ref=part.at[h, pl.ds(pl.multiple_of(c * 16, 16), 16)], dst_ref=land.at[h, col],
                 send_sem=rs_send.at[h], recv_sem=rs_recv.at[h], device_id=rs_dev(s), device_id_type=MESH).start()
         land[h, col, :, :] = part[h, pl.ds(pl.multiple_of(col * 16, 16), 16), :]
 
-    LAG = 5
-
-    @pl.loop(0, N + LAG)
+    def at(i, lag, f):
+        @pl.when((i >= lag) & (i < N + lag))
+        def _():
+            f(i - lag)
+
+    L2, L3, L4, L5, LC = LAGS
+
+    @pl.loop(0, N + LC)
     def _(i):
-        @pl.when(i < N)
-        def _():
-            first(i)
-
-        @pl.when((i >= 1) & (i < N + 1))
-        def _():
-            second(i - 1)
-
-        @pl.when((i >= 2) & (i < N + 2))
-        def _():
-            third(i - 2)
-
-        @pl.when((i >= 3) & (i < N + 3))
-        def _():
-            fourth(i - 3)
-
-        @pl.when((i >= 4) & (i < N + 4))
-        def _():
-            fifth(i - 4)
+        at(i, 0, first)
+        at(i, L2, second)
+        at(i, L3, third)
+        at(i, L4, fourth)
+        at(i, L5, fifth)
 
         @pl.when(i < M)
         def _():
             convert(i)
 
-        @pl.when(i >= LAG)
-        def _():
-            compute(i - LAG)
-
-        @pl.when(i == M - 1 + LAG)
+        at(i, LC, compute)
+
+        @pl.when(i == M - 1 + LC)
         def _():
             finish(0)
 
-        @pl.when(i == N - 1 + LAG)
+        @pl.when(i == N - 1 + LC)
         def _():
             finish(1)
 

time: 80.5 us -> 59.8 us (0.74); the launches traced: 79 us -> 59.6 us
  Pallas kernels: 77.4 us -> 58 us
    pallas_call x1, Pallas kernels: 77.4 us -> 58 us  [per_device(): pl.pallas_call(kernel, out_shape=jax.ShapeDtypeStruct((32, AB), F32), in_...]
where the time goes in v2:
time: 59.8 us; the launch traced here: 59.6 us
  Pallas kernels  58 us (97%)
  local copies, waits for them, and re-layouts  1.54 us (3%)
    pallas_call x1, Pallas kernels, per_device(): pl.pallas_call(kernel, out_shape=jax.ShapeDtypeStruct((32, AB), F32), in_...  58 us
    unnamed x1, local copies, waits for them, and re-layouts  1.54 us

profile of v2, /device:TPU:4, one launch (start us, length us, event | category | flops | bytes accessed | tf_op | source)
XLA Modules:
  0.0 59.6 jit_solution(18109892979382386228)
XLA Ops:
  0.0 58.0 %shard_map.28 = f32[32,704]{1,0:T(8,128)} custom-call(f32[1024,128]{1,0:T(8,128)} %bitcast.6, f32[704,8192]{1,0:T(8,128)} %integ.1), custom_call_target="tpu_custom_call" | custom-call | flops 2952790016 | bytes 23068672 | tf_op jit(solution)/shard_map/pallas_call | solution.py:314
  58.0 1.5 %copy.5 = f32[704,32]{0,1:T(8,128)} copy(f32[704,32]{0,1:T(8,128)} %bitcast.7) | data formatting | bytes 180224

commit v3 on v2

v3 whole, which is shorter than its diff:
```python
import functools

import jax
import jax.numpy as jnp
from jax import lax
from jax.experimental import pallas as pl
from jax.experimental.pallas import tpu as pltpu
from jax.sharding import PartitionSpec as P

MESH = pl.DeviceIdType.MESH
BF = jnp.bfloat16
F32 = jnp.float32
NT = (((1,), (1,)), ((), ()))

K = 8192
AB = 704
M = 8
CK = K // M
N = 2 * M
TILES = CK // 128
GROUPS = tuple((m, 1) for m in range(M))
PRE = 0
STAGES = 6
LAG = dict(y=3.1, xa=6.2, xb=6.3, oa=9.2, ob=9.3, x=6.2, o=9.2, y3=12.3, compute=13)
EVERY = 99


def dot(a, b):
    return lax.dot_general(a, b, NT, preferred_element_type=F32)


def split(v):
    hi = v.astype(BF)
    return hi, (v - hi.astype(F32)).astype(BF)


def kernel(amp, integ, out, raw, panel, stage, ah, al, bs, acc, part, land,
           own_sem, a2a_send, a2a_recv, stage_sem, g_send, g_recv, c_recv, rs_send, rs_recv):
    row, col = lax.axis_index("row"), lax.axis_index("col")
    core = lax.rem(row, 2)
    x = lax.rem(row // 2, 4)
    q = row // 8
    z, yhi = col // 2, lax.rem(col, 2)
    cls = lax.rem(q + yhi, 2)

    def rowid(qq, xx, kk):
        return (qq * 4 + xx) * 2 + kk

    xr, xl = lax.rem(x + 1, 4), lax.rem(x + 3, 4)
    xo = lax.rem(x + 2, 4)
    right = (rowid(q, xr, core), col)
    left = (rowid(q, xl, core), col)
    across = (rowid(1 - q, x, core), col)
    sib = (rowid(q, x, 1 - core), col)

    def a2a_dev(step):
        c = partner(step)
        return (rowid(lax.rem(cls + lax.rem(c, 2), 2), x, core), c)

    FAR_FIRST = (5, 3, 7, 1, 4, 2, 6)

    def partner(step):
        return lax.rem(z + step // 2, 4) * 2 + lax.rem(yhi + step, 2)

    def rs_dev(step):
        return (row, partner(step))

    barrier = pltpu.get_barrier_semaphore()

    def greet(dev):
        pl.semaphore_signal(barrier, inc=1, device_id=dev, device_id_type=MESH)

    for dev in (right, left, across, sib):
        greet(dev)
    for s in range(1, 8):
        greet(a2a_dev(s))
    src_slot = yhi * 4 + z

    def stage_copy(m):
        return pltpu.make_async_copy(integ.at[:, pl.ds(pl.multiple_of(m * CK, CK), CK)],
                                     stage.at[lax.rem(m, STAGES)], stage_sem.at[lax.rem(m, STAGES)])

    own_rows = pl.ds(pl.multiple_of(src_slot * 2 * TILES, 8), 2 * TILES)
    own_copy = pltpu.make_async_copy(amp.at[col], raw.at[:, own_rows], own_sem.at[0])
    own_copy.start()
    for m in range(STAGES):
        stage_copy(m).start()
    def convert(m):
        st = lax.rem(m, STAGES)
        stage_copy(m).wait()

        @pl.loop(0, AB // 16, unroll=2)
        def _(r):
            rows = pl.ds(pl.multiple_of(r * 16, 16), 16)
            hi, lo = split(stage[st, rows, :])
            ah[m, rows, :] = hi
            al[m, rows, :] = lo

        @pl.when(m + STAGES < M)
        def _():
            stage_copy(m + STAGES).start()

    pl.semaphore_wait(barrier, 11)

    for g, (m, n) in enumerate(GROUPS):
        for s in FAR_FIRST:
            pltpu.make_async_remote_copy(
                src_ref=amp.at[partner(s), pl.ds(m, n)], dst_ref=raw.at[pl.ds(m, n), own_rows],
                send_sem=a2a_send.at[0], recv_sem=a2a_recv.at[g], device_id=a2a_dev(s), device_id_type=MESH,
            ).start()

    acc[...] = jnp.zeros_like(acc)
    for m in range(PRE):
        convert(m)
    own_copy.wait()

    def slot(c, xx, kk):
        return (kk * 2 + c) * 4 + xx

    def piece(i, sl, half=None):
        rows = pl.ds(pl.multiple_of(sl * 8, 8), 8)
        if half is None:
            return panel.at[i, rows]
        return panel.at[i, rows, pl.ds(half * (CK // 2), CK // 2)]

    def send(i, sl, dev, sem, half=None):
        ref = piece(i, sl, half)
        pltpu.make_async_remote_copy(src_ref=ref, dst_ref=ref, send_sem=g_send.at[i], recv_sem=sem,
                                     device_id=dev, device_id_type=MESH).start()

    def wait(i, sl, sem):
        ref = piece(i, sl)
        pltpu.make_async_remote_copy(src_ref=ref, dst_ref=ref, send_sem=g_send.at[i], recv_sem=sem,
                                     device_id=right, device_id_type=MESH).wait_recv()

    def share(i, c):
        ref = panel.at[i, pl.ds(pl.multiple_of(slot(c, 0, core) * 8, 8), 32)]
        pltpu.make_async_remote_copy(src_ref=ref, dst_ref=ref, send_sem=g_send.at[i], recv_sem=c_recv.at[i],
                                     device_id=sib, device_id_type=MESH).start()

    own = slot(cls, x, core)

    def y_first(i):
        return (core == 0) | (lax.rem(i, EVERY) == EVERY - 1)

    def x_first(i):
        return (core == 1) & (lax.rem(i, EVERY) != EVERY - 1)

    def first(i):
        m = i
        for g, (m0, n) in enumerate(GROUPS):
            @pl.when(i == m0)
            def _():
                ref = raw.at[pl.ds(m0, n), pl.ds(0, 7 * 2 * TILES)]
                pltpu.make_async_remote_copy(src_ref=ref, dst_ref=ref, send_sem=a2a_send.at[0], recv_sem=a2a_recv.at[g],
                                             device_id=right, device_id_type=MESH).wait_recv()

        @pl.when(i < M)
        def _():
            for t in range(TILES):
                for j in range(2):
                    panel[m + j * M, pl.ds(pl.multiple_of(own * 8, 8), 8), t * 128:(t + 1) * 128] = (
                        raw[m, pl.ds(2 * t + j, 8, stride=2 * TILES), :])

        send(i, own, right, g_recv.at[i, 0])
        send(i, own, left, g_recv.at[i, 1])
        send(i, own, across, g_recv.at[i, 2])

    def from_sides(i, c, s, fwd, on_across):
        for xx, dev, k in ((xl, right, 0), (xr, left, 1)):
            wait(i, slot(c, xx, core), g_recv.at[i, s + k])
            send(i, slot(c, xx, core), dev, g_recv.at[i, fwd], k)
            if on_across:
                send(i, slot(c, xx, core), across, g_recv.at[i, 4 + k])

    def y_theirs(i):
        theirs = slot(1 - cls, x, core)
        wait(i, theirs, g_recv.at[i, 2])
        send(i, theirs, right, g_recv.at[i, 3])
        send(i, theirs, left, g_recv.at[i, 4])

    def y_sides_own(i):
        from_sides(i, cls, 0, 5, False)

    def y_sides_theirs(i):
        from_sides(i, 1 - cls, 3, 6, False)

    def y_far_own(i):
        wait(i, slot(cls, xo, core), g_recv.at[i, 5])
        share(i, cls)

    def y_far_theirs(i):
        wait(i, slot(1 - cls, xo, core), g_recv.at[i, 6])
        share(i, 1 - cls)

    def x_sides(i):
        from_sides(i, cls, 0, 3, True)

    def x_far(i):
        wait(i, slot(cls, xo, core), g_recv.at[i, 3])
        send(i, slot(cls, xo, core), across, g_recv.at[i, 6])
        share(i, cls)

    def x_theirs(i):
        for xx, k in ((x, 2), (xl, 4), (xr, 5), (xo, 6)):
            wait(i, slot(1 - cls, xx, core), g_recv.at[i, k])
        share(i, 1 - cls)

    def compute(i):
        m = lax.rem(i, M)
        ref = panel.at[i, pl.ds(0, 64)]
        pltpu.make_async_remote_copy(src_ref=ref, dst_ref=ref, send_sem=g_send.at[i], recv_sem=c_recv.at[i],
                                     device_id=sib, device_id_type=MESH).wait_recv()
        mask = lax.rem(lax.broadcasted_iota(jnp.int32, (16, CK), 0), 8) < 4
        for xx in range(4):
            v0, v1 = (jnp.concatenate([panel[i, slot(c, xx, kk) * 8:slot(c, xx, kk) * 8 + 8, :] for kk in range(2)], 0)
                      for c in range(2))
            for y, v in ((0, jnp.where(mask, v0, v1)), (1, jnp.where(mask, v1, v0))):
                hi, lo = split(v)
                at = y * 64 + xx * 16
                bs[at:at + 16, :] = hi
                bs[128 + at:128 + at + 16, :] = lo
        for a0, a1 in ((0, 704),):
            acc[a0:a1, :] += dot(ah[m, a0:a1, :], bs[...])
            acc[a0:a1, 0:128] += dot(al[m, a0:a1, :], bs[0:128, :])

    def finish(h, _):
        part[h, :, :] = (acc[:, 0:128] + acc[:, 128:256]).T
        for s in FAR_FIRST:
            c = partner(s)
            pltpu.make_async_remote_copy(
                src_ref=part.at[h, pl.ds(pl.multiple_of(c * 16, 16), 16)], dst_ref=land.at[h, col],
                send_sem=rs_send.at[h], recv_sem=rs_recv.at[h], device_id=rs_dev(s), device_id_type=MESH).start()
        land[h, col, :, :] = part[h, pl.ds(pl.multiple_of(col * 16, 16), 16), :]
        if h == 0:
            acc[...] = jnp.zeros_like(acc)

    always = lambda i: True
    work = sorted([
        (0.0, first, always), (LAG["y"], y_theirs, y_first), (LAG["xa"], y_sides_own, y_first),
        (LAG["xb"], y_sides_theirs, y_first), (LAG["oa"], y_far_own, y_first), (LAG["ob"], y_far_theirs, y_first),
        (LAG["x"], x_sides, x_first), (LAG["o"], x_far, x_first), (LAG["y3"], x_theirs, x_first),
    ], key=lambda item: item[0] % 1)
    LC = int(LAG["compute"])

    def at(step, lag, f, role):
        i = step - lag

        @pl.when((i >= 0) & (i < N) & role(i))
        def _():
            f(i)

    @pl.loop(0, N + LC)
    def _(step):
        for lag, f, role in work:
            at(step, int(lag), f, role)

        @pl.when(step < M)
        def _():
            convert(step)

        at(step, LC, compute, always)
        for h in range(2):
            at(step, LC, functools.partial(finish, h), lambda i: i == h * M + M - 1)

    for h in range(2):
        ref = land.at[h, pl.ds(0, 7)]
        pltpu.make_async_remote_copy(src_ref=ref, dst_ref=ref, send_sem=rs_send.at[h], recv_sem=rs_recv.at[h],
                                     device_id=right, device_id_type=MESH).wait_recv()
        total = land[h, 0]
        for c in range(1, 8):
            total += land[h, c]
        total = 0.5 * total
        for kk in range(2):
            for yy in range(2):
                for zz in range(4):
                    r = kk * 16 + zz * 4 + yy * 2 + h
                    s = kk * 8 + yy * 4 + zz
                    out[r:r + 1, :] = total[s:s + 1, :]

    ref = raw.at[:, pl.ds(0, 7 * 2 * TILES)]
    pltpu.make_async_remote_copy(src_ref=ref, dst_ref=ref, send_sem=a2a_send.at[0], recv_sem=a2a_recv.at[0],
                                 device_id=right, device_id_type=MESH).wait_send()

    @pl.loop(0, N)
    def _(i):
        ref = panel.at[i, pl.ds(0, 120)]
        pltpu.make_async_remote_copy(src_ref=ref, dst_ref=ref, send_sem=g_send.at[i], recv_sem=c_recv.at[i],
                                     device_id=right, device_id_type=MESH).wait_send()

    for h in range(2):
        ref = land.at[h, pl.ds(0, 7)]
        pltpu.make_async_remote_copy(src_ref=ref, dst_ref=ref, send_sem=rs_send.at[h], recv_sem=rs_recv.at[h],
                                     device_id=right, device_id_type=MESH).wait_send()


def per_device(amplitudes, integrals):
    amp = amplitudes.reshape(512, 128, 2).transpose(0, 2, 1).reshape(8, M, 2 * TILES, 128)
    dma = pltpu.SemaphoreType.DMA
    out = pl.pallas_call(
        kernel,
        out_shape=jax.ShapeDtypeStruct((32, AB), F32),
        in_specs=[pl.BlockSpec(memory_space=pl.ANY)] * 2,
        out_specs=pl.BlockSpec(memory_space=pltpu.VMEM),
        scratch_shapes=[
            pltpu.VMEM((M, 8 * 2 * TILES, 128), F32),
            pltpu.VMEM((N, 128, CK), F32),
            pltpu.VMEM((STAGES, AB, CK), F32),
            pltpu.VMEM((M, AB, CK), BF),
            pltpu.VMEM((M, AB, CK), BF),
            pltpu.VMEM((256, CK), BF),
            pltpu.VMEM((AB, 256), F32),
            pltpu.VMEM((2, 128, AB), F32),
            pltpu.VMEM((2, 8, 16, AB), F32),
            dma((1,)), dma((1,)), dma((len(GROUPS),)), dma((STAGES,)),
            dma((N,)), dma((N, 7)), dma((N,)), dma((2,)), dma((2,)),
        ],
        compiler_params=pltpu.CompilerParams(collective_id=0, has_side_effects=True, vmem_limit_bytes=60 * 2**20),
        cost_estimate=pl.CostEstimate(flops=2 * AB * K * 256, bytes_accessed=4 * AB * K, transcendentals=0),
    )(amp, integrals)
    return out.T


def solution(mesh):
    return jax.shard_map(
        per_device,
        mesh=mesh,
        in_specs=(P(None, ("row", "col")), P("row", "col")),
        out_specs=P("row", "col"),
        check_vma=False,
    )
```

time: 59.8 us -> 59.3 us (level)
  no operation moved by 1% of the time
where the time goes in v3:
time: 59.3 us; the launch traced here: 59.2 us
  Pallas kernels  57.7 us (97%)
  local copies, waits for them, and re-layouts  1.54 us (3%)
    pallas_call x1, Pallas kernels, per_device(): pl.pallas_call(kernel, out_shape=jax.ShapeDtypeStruct((32, AB), F32), in_...  57.7 us
    unnamed x1, local copies, waits for them, and re-layouts  1.54 us

profile of v3, /device:TPU:4, one launch (start us, length us, event | category | flops | bytes accessed | tf_op | source)
XLA Modules:
  0.0 59.2 jit_solution(14783361926901345112)
XLA Ops:
  0.0 57.7 %shard_map.28 = f32[32,704]{1,0:T(8,128)} custom-call(f32[8,8,16,128]{3,2,1,0:T(8,128)} %bitcast.6, f32[704,8192]{1,0:T(8,128)} %integ.1), custom_call_target="tpu_custom_call" | custom-call | flops 2952790016 | bytes 23068672 | tf_op jit(solution)/shard_map/pallas_call | solution.py:300
  57.7 1.5 %copy.5 = f32[704,32]{0,1:T(8,128)} copy(f32[704,32]{0,1:T(8,128)} %bitcast.7) | data formatting | bytes 180224

commit v4 on v3

--- a/solution.py
+++ b/solution.py
@@ -299,7 +299,7 @@
     dma = pltpu.SemaphoreType.DMA
     out = pl.pallas_call(
         kernel,
-        out_shape=jax.ShapeDtypeStruct((32, AB), F32),
+        out_shape=pltpu.VMEM((32, AB), F32),
         in_specs=[pl.BlockSpec(memory_space=pl.ANY)] * 2,
         out_specs=pl.BlockSpec(memory_space=pltpu.VMEM),
         scratch_shapes=[

time: 59.3 us -> 57.8 us (0.975)
  local copies, waits for them, and re-layouts: 1.54 us -> 0.64 us
  Pallas kernels: 57.7 us -> 57 us
    unnamed x1, local copies, waits for them, and re-layouts: 1.54 us -> 0.64 us
    pallas_call x1, Pallas kernels: 57.7 us -> 57 us  [per_device(): pl.pallas_call(kernel, out_shape=pltpu.VMEM((32, AB), F32), in_specs=[pl....]
where the time goes in v4:
time: 57.8 us; the launch traced here: 57.7 us
  Pallas kernels  57 us (99%)
  local copies, waits for them, and re-layouts  0.64 us (1%)
    pallas_call x1, Pallas kernels, per_device(): pl.pallas_call(kernel, out_shape=pltpu.VMEM((32, AB), F32), in_specs=[pl....  57 us

profile of v4, /device:TPU:4, one launch (start us, length us, event | category | flops | bytes accessed | tf_op | source)
XLA Modules:
  0.0 57.7 jit_solution(121298984009021804)
XLA Ops:
  0.0 57.0 %shard_map.28 = f32[32,704]{1,0:T(8,128)S(1)} custom-call(f32[8,8,16,128]{3,2,1,0:T(8,128)} %bitcast.7, f32[704,8192]{1,0:T(8,128)} %integ.1), custom_call_target="tpu_custom_call" | custom-call | flops 2952790016 | bytes 23068672 | tf_op jit(solution)/shard_map/pallas_call | solution.py:300
  57.0 0.6 %copy.5 = f32[704,32]{0,1:T(8,128)} copy(f32[704,32]{0,1:T(8,128)S(1)} %bitcast.6) | data formatting | bytes 180224

commit v5 on v4

--- a/solution.py
+++ b/solution.py
@@ -21,7 +21,7 @@
 GROUPS = tuple((m, 1) for m in range(M))
 PRE = 0
 STAGES = 6
-LAG = dict(y=3.1, xa=6.2, xb=6.3, oa=9.2, ob=9.3, x=6.2, o=9.2, y3=12.3, compute=13)
+LAG = dict(y=4.1, xa=7.2, xb=7.3, oa=10.2, ob=10.3, x=6.2, o=9.2, y3=13.3, compute=14)
 EVERY = 99
 
 

time: 57.8 us -> 57.4 us (level)
  Pallas kernels: 57 us -> 56.4 us
    pallas_call x1, Pallas kernels: 57 us -> 56.4 us  [per_device(): pl.pallas_call(kernel, out_shape=pltpu.VMEM((32, AB), F32), in_specs=[pl....]
where the time goes in v5:
time: 57.4 us; the launch traced here: 57 us
  Pallas kernels  56.4 us (98%)
  local copies, waits for them, and re-layouts  0.64 us (1%)
    pallas_call x1, Pallas kernels, per_device(): pl.pallas_call(kernel, out_shape=pltpu.VMEM((32, AB), F32), in_specs=[pl....  56.4 us

profile of v5, /device:TPU:4, one launch (start us, length us, event | category | flops | bytes accessed | tf_op | source)
XLA Modules:
  0.0 57.0 jit_solution(10048268889613435631)
XLA Ops:
  0.0 56.4 %shard_map.28 = f32[32,704]{1,0:T(8,128)S(1)} custom-call(f32[8,8,16,128]{3,2,1,0:T(8,128)} %bitcast.7, f32[704,8192]{1,0:T(8,128)} %integ.1), custom_call_target="tpu_custom_call" | custom-call | flops 2952790016 | bytes 23068672 | tf_op jit(solution)/shard_map/pallas_call | solution.py:300
  56.4 0.6 %copy.5 = f32[704,32]{0,1:T(8,128)} copy(f32[704,32]{0,1:T(8,128)S(1)} %bitcast.6) | data formatting | bytes 180224

commit v6 on v5

--- a/solution.py
+++ b/solution.py
@@ -221,11 +221,11 @@
                 bs[at:at + 16, :] = hi
                 bs[128 + at:128 + at + 16, :] = lo
         for a0, a1 in ((0, 704),):
-            acc[a0:a1, :] += dot(ah[m, a0:a1, :], bs[...])
-            acc[a0:a1, 0:128] += dot(al[m, a0:a1, :], bs[0:128, :])
+            both = dot(ah[m, a0:a1, :], bs[...])
+            acc[a0:a1, :] += both[:, 0:128] + both[:, 128:256] + dot(al[m, a0:a1, :], bs[0:128, :])
 
     def finish(h, _):
-        part[h, :, :] = (acc[:, 0:128] + acc[:, 128:256]).T
+        part[h, :, :] = acc[...].T
         for s in FAR_FIRST:
             c = partner(s)
             pltpu.make_async_remote_copy(
@@ -309,7 +309,7 @@
             pltpu.VMEM((M, AB, CK), BF),
             pltpu.VMEM((M, AB, CK), BF),
             pltpu.VMEM((256, CK), BF),
-            pltpu.VMEM((AB, 256), F32),
+            pltpu.VMEM((AB, 128), F32),
             pltpu.VMEM((2, 128, AB), F32),
             pltpu.VMEM((2, 8, 16, AB), F32),
             dma((1,)), dma((1,)), dma((len(GROUPS),)), dma((STAGES,)),

time: 57.4 us -> 57.5 us (level)
  no operation moved by 1% of the time
where the time goes in v6:
time: 57.5 us; the launch traced here: 57 us
  Pallas kernels  56.4 us (98%)
  local copies, waits for them, and re-layouts  0.64 us (1%)
    pallas_call x1, Pallas kernels, per_device(): pl.pallas_call(kernel, out_shape=pltpu.VMEM((32, AB), F32), in_specs=[pl....  56.4 us

profile of v6, /device:TPU:4, one launch (start us, length us, event | category | flops | bytes accessed | tf_op | source)
XLA Modules:
  0.0 57.0 jit_solution(4124694012862890232)
XLA Ops:
  0.0 56.4 %shard_map.28 = f32[32,704]{1,0:T(8,128)S(1)} custom-call(f32[8,8,16,128]{3,2,1,0:T(8,128)} %bitcast.7, f32[704,8192]{1,0:T(8,128)} %integ.1), custom_call_target="tpu_custom_call" | custom-call | flops 2952790016 | bytes 23068672 | tf_op jit(solution)/shard_map/pallas_call | solution.py:300
  56.4 0.6 %copy.5 = f32[704,32]{0,1:T(8,128)} copy(f32[704,32]{0,1:T(8,128)S(1)} %bitcast.6) | data formatting | bytes 180224
